TPU v7x, 32 devices: a whole 2x2x4 slice. The times are simulated.
32 devices in a mesh: sub: 16 (over z, y, x), face: 2 (over core).
Axes of the slice: x: 2, y: 2, z: 4, core: 2. Of those that a mesh axis runs over, the one named last changes fastest.
Arguments:
- schur_blocks: float32 [16, 1024, 1024], P('sub', 'face'), may hold values from -1 to 4, as said below
- rigid_body_modes: float32 [16, 6, 1024], P('sub', None, 'face'), may hold values from -1 to 1
- load_cases: float32 [16, 1024, 128], P('sub', 'face'), may hold values from -60 to 60
- face_sizes: int32 [16, 4], P('sub', 'face'), may hold values from 128 to 256
- contact_mask: int32 [16, 1024], P('sub', 'face'), may hold values 0 or 1
- friction_mask: int32 [16, 1024], P('sub', 'face'), may hold values 0 or 1
- cluster_ids: int32 [16], P('sub'), may hold values from 0 to 1, as said below
- pairing: int32 [16, 2, 2, 1], P('sub', 'face'), may hold values from 0 to 0, as said below
Outputs:
- multipliers: float32 [16, 1024, 128], P('sub', 'face')
- residual: float32 [16, 1024, 128], P('sub', 'face')
Inputs may be any that keep to these rules, and one draw needn't show every extreme that they name: `schur_blocks`: each block is symmetric and positive definite. `cluster_ids`: every cluster number names exactly 8 subdomains. Each device holds one subdomain, so every pairing entry is 0 (the identity matching); pairing[(i + 1) mod 16, c, 1, pairing[i, c, 0, g]] = g holds trivially.
All inputs are finite; a program needn't handle non-finite values. No bound on the sum of `contact_mask` or of `friction_mask` on one device may be relied on, other than what follows from the above.
Results may differ from a plain program's by a relative error of at most 0.00025.
Values sent between devices are 32-bit elements; how exact they have to be, the bound alone decides.
A program may use at most 64 MiB of HBM per device.

v0:
```python
import jax
import jax.numpy as jnp
from jax import lax
from jax.sharding import PartitionSpec as P

ITERS = 2


HIGH_ACCURACY = lax.Precision.HIGHEST


def passed_along(value, axis, steps):
    count = lax.axis_size(axis)
    pairs = [(source, (source + steps) % count) for source in range(count)]
    return lax.ppermute(value, axis, pairs)


def coarse_inverse(coarse_gram):
    lower_factor = jnp.linalg.cholesky(coarse_gram)
    eye_block = jnp.broadcast_to(
        jnp.eye(coarse_gram.shape[1], dtype=coarse_gram.dtype), coarse_gram.shape
    )
    inverse_factor = lax.linalg.triangular_solve(
        lower_factor, eye_block, left_side=True, lower=True
    )
    return jnp.einsum("bkm,bkn->bmn", inverse_factor, inverse_factor, precision=HIGH_ACCURACY)


def on_device(
    schur_blocks,
    rigid_body_modes,
    load_cases,
    face_sizes,
    contact_mask,
    friction_mask,
    cluster_ids,
    pairing,
):
    sub_count, row_count, width = schur_blocks.shape
    columns = load_cases.shape[2]
    face_len = row_count // 2
    clusters = sub_count * lax.axis_size("sub") // 8
    positions = jnp.arange(face_len, dtype=jnp.int32)
    inside = (
        (positions[None, None, :] < face_sizes[:, :, None])
        .astype(jnp.float32)
        .reshape(sub_count, row_count)
    )
    blocked = (contact_mask * (1 - friction_mask)).astype(jnp.float32)
    free_mask = (inside * (1.0 - blocked))[:, :, None]
    choice_matrix = (cluster_ids[:, None] == jnp.arange(clusters, dtype=jnp.int32)[None, :]).astype(
        jnp.float32
    )
    face_sign = (1 - 2 * (jnp.arange(row_count, dtype=jnp.int32) // face_len)).astype(jnp.float32)[
        None, :, None
    ]
    pair_right = pairing[0, 0, 0]
    pair_left = pairing[0, 0, 1]

    def partial_coarse(entry_values):
        subdomain_part = jnp.einsum(
            "hxy,hyj->hxj", rigid_body_modes, entry_values, precision=HIGH_ACCURACY
        )
        return jnp.einsum("fo,flu->olu", choice_matrix, subdomain_part, precision=HIGH_ACCURACY)

    local_gram = jnp.einsum(
        "gmk,gnk->gmn", rigid_body_modes, rigid_body_modes, precision=HIGH_ACCURACY
    )
    gram_part = jnp.einsum("gb,gmn->bmn", choice_matrix, local_gram, precision=HIGH_ACCURACY)
    masked_loads = free_mask * load_cases
    coarse_gram, coarse_first = lax.psum((gram_part, partial_coarse(masked_loads)), ("sub", "face"))
    inverse = coarse_inverse(coarse_gram)

    def correct(entry_values, coarse):
        weight_factors = jnp.einsum("bmn,bnr->bmr", inverse, coarse, precision=HIGH_ACCURACY)
        scatter_copies = jnp.einsum(
            "wc,cis->wis", choice_matrix, weight_factors, precision=HIGH_ACCURACY
        )
        return entry_values - jnp.einsum(
            "fpd,fpx->fdx", rigid_body_modes, scatter_copies, precision=HIGH_ACCURACY
        )

    def partner(entry_values):
        shaped = entry_values.reshape(sub_count, 2, face_len, columns)
        from_right = passed_along(shaped[:, 1], "sub", -1)
        from_left = passed_along(shaped[:, 0], "sub", 1)
        matched = jnp.stack(
            [jnp.take(from_right, pair_right, axis=0), jnp.take(from_left, pair_left, axis=0)],
            axis=1,
        )
        return matched.reshape(entry_values.shape)

    def squares(entry_values):
        return lax.psum(jnp.sum(entry_values * entry_values, axis=(0, 1)), ("sub", "face"))

    residual = free_mask * correct(masked_loads, coarse_first)
    direction = residual
    norm_now = squares(residual)
    multipliers = jnp.zeros_like(load_cases)
    for iteration in range(ITERS):
        masked_dir = free_mask * direction
        coarse_in = lax.psum(partial_coarse(masked_dir), ("sub", "face"))
        projected = correct(masked_dir, coarse_in)
        joined = face_sign * (projected + partner(projected))
        signed = face_sign * jnp.einsum(
            "gkc,gcr->gkr",
            schur_blocks,
            lax.all_gather(joined, "face", axis=1, tiled=True),
            precision=HIGH_ACCURACY,
        )
        folded = signed + partner(signed)
        local_curv = jnp.sum(projected * folded, axis=(0, 1))
        coarse_out, curvature = lax.psum((partial_coarse(folded), local_curv), ("sub", "face"))
        image = free_mask * correct(folded, coarse_out)
        step_size = norm_now / curvature
        multipliers = multipliers + step_size * direction
        residual = residual - step_size * image
        if iteration + 1 < ITERS:
            norm_next = squares(residual)
            ratio = norm_next / norm_now
            direction = residual + ratio * direction
            norm_now = norm_next
    return (multipliers, residual)


def solution(mesh):
    placed = (
        P("sub", "face", None),
        P("sub", None, "face"),
        P("sub", "face", None),
        P("sub", "face"),
        P("sub", "face"),
        P("sub", "face"),
        P("sub"),
        P("sub", "face", None, None),
    )
    return jax.shard_map(
        on_device,
        mesh=mesh,
        in_specs=placed,
        out_specs=(P("sub", "face", None), P("sub", "face", None)),
        check_vma=False,
    )
```

profile of v0, /device:TPU:0, one launch (start us, length us, event | category | flops | bytes accessed | tf_op | source)
XLA Modules:
  0.0 314.0 jit_solution(1295220982557252766)
XLA Ops:
  1.5 0.7 broadcast_bitcast_fusion
  2.2 0.9 fusion.61
  3.1 1.1 copy.31
  4.3 0.7 compare_select_fusion
  5.0 1.0 convolution_bitcast_fusion.9
  6.1 42.2 %all-reduce.2 = (f32[2,6,6]{1,2,0:T(8,128)S(1)}, f32[2,6,128]{2,1,0:T(8,128)S(1)}) all-reduce(f32[2,6,6]{1,2,0:T(8,128)S(1)} %broadcast_multiply_fusion.5, f32[2,6,128]{2,1,0:T(8,128)S(1)} %broadcast_multiply_fusion.4), channel_id=1, replica_groups=mesh['sub'=16,'face'=2] {'sub','face'}, use_global_device_ids=true, to_apply=%region_0.1 | all-reduce | flops 1608 | bytes 12864 | tf_op jit(solution)/shard_map/psum | solution.py:71
  48.4 1.1 custom-call.7
  49.7 1.0 custom-call.8
  50.6 0.2 fusion.74
  51.0 0.1 fusion.118
  51.1 0.1 fusion.85
  51.3 1.2 multiply_reduce_fusion.1
  52.5 1.0 convolution_bitcast_fusion.8
  53.6 40.2 %psum.73 = f32[2,6,128]{2,1,0:T(8,128)S(1)} all-reduce(f32[2,6,128]{2,1,0:T(8,128)S(1)} %broadcast_multiply_fusion.3), channel_id=1, replica_groups=mesh['sub'=16,'face'=2] {'sub','face'}, use_global_device_ids=true, to_apply=%region_6.7 | all-reduce | flops 1536 | bytes 12288 | tf_op jit(solution)/shard_map/psum | solution.py:102
  93.9 0.1 fusion.83
  94.1 1.2 fusion.26
  95.2 0.2 reshape.358
  95.4 0.2 slice_bitcast_fusion.7
  95.6 4.9 %collective-permute-start = (f32[1,256,128]{1,0,2:T(1,128)S(1)}, f32[1,256,128]{1,0,2:T(1,128)S(1)}, u32[]{:S(2)}, u32[]{:S(2)}) collective-permute-start(f32[1,256,128]{1,0,2:T(1,128)S(1)} %get-tuple-element.23), channel_id=1, source_target_pairs={{0,30},{2,0},{4,2},{6,4},{8,6},{10,8},{12,10},{14,12},{16,14},{18,... | collective-permute-start | bytes 393224 | tf_op jit(solution)/shard_map/ppermute | solution.py:15
  100.6 0.7 fusion.116
  105.4 3.7 %collective-permute-done.1 = f32[1,256,128]{1,0,2:T(1,128)S(1)} collective-permute-done((f32[1,256,128]{1,0,2:T(1,128)S(1)}, f32[1,256,128]{1,0,2:T(1,128)S(1)}, u32[]{:S(2)}, u32[]{:S(2)}) %collective-permute-start.1) | collective-permute-done | bytes 131104 | tf_op jit(solution)/shard_map/ppermute | solution.py:15
  109.2 0.2 pad_maximum_fusion
  109.5 0.2 copy.40
  109.7 0.2 reshape.359
  109.9 2.2 all_gather.6
  112.1 2.2 fusion.7
  114.4 0.2 reshape.362
  114.6 0.2 slice_bitcast_fusion.5
  114.8 2.0 collective-permute-start.2
  116.9 4.3 %collective-permute-done.2 = f32[1,256,128]{1,0,2:T(1,128)S(1)} collective-permute-done((f32[1,256,128]{1,0,2:T(1,128)S(1)}, f32[1,256,128]{1,0,2:T(1,128)S(1)}, u32[]{:S(2)}, u32[]{:S(2)}) %collective-permute-start.2) | collective-permute-done | bytes 131104 | tf_op jit(solution)/shard_map/ppermute | solution.py:15
  121.3 4.3 %collective-permute-done.3 = f32[1,256,128]{1,0,2:T(1,128)S(1)} collective-permute-done((f32[1,256,128]{1,0,2:T(1,128)S(1)}, f32[1,256,128]{1,0,2:T(1,128)S(1)}, u32[]{:S(2)}, u32[]{:S(2)}) %collective-permute-start.3) | collective-permute-done | bytes 131104 | tf_op jit(solution)/shard_map/ppermute | solution.py:15
  125.7 0.2 pad_maximum_fusion.1
  126.0 0.2 copy.43
  126.2 0.1 fusion.34
  126.3 0.3 convolution_bitcast_fusion.7
  126.7 37.0 %all-reduce.1 = (f32[128]{0:T(128)S(1)}, f32[128]{0:T(128)S(1)}, f32[2,6,128]{2,1,0:T(8,128)S(1)}) all-reduce(f32[128]{0:T(128)S(1)} %get-tuple-element.27, f32[128]{0:T(128)S(1)} %get-tuple-element.15, f32[2,6,128]{2,1,0:T(8,128)S(1)} %broadcast_multiply_fusion.2), channel_id=1, replica_groups=mesh['sub'=16,'face'=2] {'sub','face'}, use_global_device_ids=true, to_apply=%region_5.6 | all-reduce | flops 1792 | bytes 14336 | tf_op jit(solution)/shard_map/psum | solution.py:94
  163.9 0.1 fusion.81
  164.0 0.5 multiply_reduce_fusion
  164.5 41.0 %psum.76 = f32[128]{0:T(128)S(1)} all-reduce(f32[128]{0:T(128)S(1)} %get-tuple-element.29), channel_id=1, replica_groups=mesh['sub'=16,'face'=2] {'sub','face'}, use_global_device_ids=true, to_apply=%region_11.12 | all-reduce | flops 128 | bytes 1024 | tf_op jit(solution)/shard_map/psum | solution.py:94
  205.5 0.4 convolution_bitcast_fusion.6
  206.0 39.9 %psum.77 = f32[2,6,128]{2,1,0:T(8,128)S(1)} all-reduce(f32[2,6,128]{2,1,0:T(8,128)S(1)} %broadcast_multiply_fusion.1), channel_id=1, replica_groups=mesh['sub'=16,'face'=2] {'sub','face'}, use_global_device_ids=true, to_apply=%region_12.13 | all-reduce | flops 1536 | bytes 12288 | tf_op jit(solution)/shard_map/psum | solution.py:102
  246.1 0.4 fusion.27
  246.6 0.2 reshape.365
  246.7 0.2 slice_bitcast_fusion.3
  246.9 3.2 %collective-permute-start.4 = (f32[1,256,128]{1,0,2:T(1,128)S(1)}, f32[1,256,128]{1,0,2:T(1,128)S(1)}, u32[]{:S(2)}, u32[]{:S(2)}) collective-permute-start(f32[1,256,128]{1,0,2:T(1,128)S(1)} %get-tuple-element.19), channel_id=1, source_target_pairs={{0,30},{2,0},{4,2},{6,4},{8,6},{10,8},{12,10},{14,12},{16,14},{18,... | collective-permute-start | bytes 393224 | tf_op jit(solution)/shard_map/ppermute | solution.py:15
  250.1 3.1 %collective-permute-done.4 = f32[1,256,128]{1,0,2:T(1,128)S(1)} collective-permute-done((f32[1,256,128]{1,0,2:T(1,128)S(1)}, f32[1,256,128]{1,0,2:T(1,128)S(1)}, u32[]{:S(2)}, u32[]{:S(2)}) %collective-permute-start.4) | collective-permute-done | bytes 131104 | tf_op jit(solution)/shard_map/ppermute | solution.py:15
  253.4 5.3 %collective-permute-done.5 = f32[1,256,128]{1,0,2:T(1,128)S(1)} collective-permute-done((f32[1,256,128]{1,0,2:T(1,128)S(1)}, f32[1,256,128]{1,0,2:T(1,128)S(1)}, u32[]{:S(2)}, u32[]{:S(2)}) %collective-permute-start.5) | collective-permute-done | bytes 131104 | tf_op jit(solution)/shard_map/ppermute | solution.py:15
  258.8 0.2 pad_maximum_fusion.2
  259.0 0.2 reshape.366
  259.3 2.2 all_gather.7
  261.5 2.2 fusion.13
  263.7 0.2 reshape.368
  263.9 0.2 slice_bitcast_fusion.1
  264.1 0.2 collective-permute-start.6
  264.4 1.8 collective-permute-start.7
  266.2 4.3 %collective-permute-done.6 = f32[1,256,128]{1,0,2:T(1,128)S(1)} collective-permute-done((f32[1,256,128]{1,0,2:T(1,128)S(1)}, f32[1,256,128]{1,0,2:T(1,128)S(1)}, u32[]{:S(2)}, u32[]{:S(2)}) %collective-permute-start.6) | collective-permute-done | bytes 131104 | tf_op jit(solution)/shard_map/ppermute | solution.py:15
  270.6 2.7 collective-permute-done.7
  273.5 0.2 pad_maximum_fusion.3
  273.7 0.2 copy.49
  274.1 0.3 convolution_bitcast_fusion.5
  274.5 37.0 %all-reduce = (f32[128]{0:T(128)S(1)}, f32[2,6,128]{2,1,0:T(8,128)S(1)}) all-reduce(f32[128]{0:T(128)S(1)} %get-tuple-element.13, f32[2,6,128]{2,1,0:T(8,128)S(1)} %broadcast_multiply_fusion), channel_id=1, replica_groups=mesh['sub'=16,'face'=2] {'sub','face'}, use_global_device_ids=true, to_apply=%region_14.15 | all-reduce | flops 1664 | bytes 13312 | tf_op jit(solution)/shard_map/psum | solution.py:113
  311.6 0.8 copy.50
  312.7 0.5 fusion.29
  313.2 0.8 copy.51
  (53 shorter events, 3.2 us)
Async XLA Ops:
  0.6 111.5 %copy-start = (f32[1,512,1024]{2,1,0:T(8,128)S(1)}, f32[1,512,1024]{2,1,0:T(8,128)}, u32[]{:S(2)}) copy-start(f32[1,512,1024]{2,1,0:T(8,128)} %param.8) | copy-start | bytes 6291460
  0.6 99.9 %copy-start.2 = (s32[1,1,2,1]{2,3,1,0:T(1,128)S(1)}, s32[1,1,2,1]{2,3,1,0:T(1,128)}, u32[]{:S(2)}) copy-start(s32[1,1,2,1]{2,3,1,0:T(1,128)} %param.15) | copy-start | bytes 28
  95.6 9.6 %collective-permute-start = (f32[1,256,128]{1,0,2:T(1,128)S(1)}, f32[1,256,128]{1,0,2:T(1,128)S(1)}, u32[]{:S(2)}, u32[]{:S(2)}) collective-permute-start(f32[1,256,128]{1,0,2:T(1,128)S(1)} %get-tuple-element.23), channel_id=1, source_target_pairs={{0,30},{2,0},{4,2},{6,4},{8,6},{10,8},{12,10},{14,12},{16,14},{18,... | collective-permute-start | bytes 393224 | tf_op jit(solution)/shard_map/ppermute | solution.py:15
  100.6 8.6 %collective-permute-start.1 = (f32[1,256,128]{1,0,2:T(1,128)S(1)}, f32[1,256,128]{1,0,2:T(1,128)S(1)}, u32[]{:S(2)}, u32[]{:S(2)}) collective-permute-start(f32[1,256,128]{1,0,2:T(1,128)S(1)} %get-tuple-element.24), channel_id=1, source_target_pairs={{0,2},{2,4},{4,6},{6,8},{8,10},{10,12},{12,14},{14,16},{16,18},{18... | collective-permute-start | bytes 393224 | tf_op jit(solution)/shard_map/ppermute | solution.py:15
  114.4 12.0 %copy-start.1 = (f32[1,6,512]{2,0,1:T(1,128)S(1)}, f32[1,6,512]{2,0,1:T(1,128)}, u32[]{:S(2)}) copy-start(f32[1,6,512]{2,0,1:T(1,128)} %param.9) | copy-start | bytes 36868
  114.8 6.4 %collective-permute-start.2 = (f32[1,256,128]{1,0,2:T(1,128)S(1)}, f32[1,256,128]{1,0,2:T(1,128)S(1)}, u32[]{:S(2)}, u32[]{:S(2)}) collective-permute-start(f32[1,256,128]{1,0,2:T(1,128)S(1)} %get-tuple-element.21), channel_id=1, source_target_pairs={{0,30},{2,0},{4,2},{6,4},{8,6},{10,8},{12,10},{14,12},{16,14},{18,... | collective-permute-start | bytes 393224 | tf_op jit(solution)/shard_map/ppermute | solution.py:15
  116.7 8.9 %collective-permute-start.3 = (f32[1,256,128]{1,0,2:T(1,128)S(1)}, f32[1,256,128]{1,0,2:T(1,128)S(1)}, u32[]{:S(2)}, u32[]{:S(2)}) collective-permute-start(f32[1,256,128]{1,0,2:T(1,128)S(1)} %get-tuple-element.22), channel_id=1, source_target_pairs={{0,2},{2,4},{4,6},{6,8},{8,10},{10,12},{12,14},{14,16},{16,18},{18... | collective-permute-start | bytes 393224 | tf_op jit(solution)/shard_map/ppermute | solution.py:15
  246.9 6.3 %collective-permute-start.4 = (f32[1,256,128]{1,0,2:T(1,128)S(1)}, f32[1,256,128]{1,0,2:T(1,128)S(1)}, u32[]{:S(2)}, u32[]{:S(2)}) collective-permute-start(f32[1,256,128]{1,0,2:T(1,128)S(1)} %get-tuple-element.19), channel_id=1, source_target_pairs={{0,30},{2,0},{4,2},{6,4},{8,6},{10,8},{12,10},{14,12},{16,14},{18,... | collective-permute-start | bytes 393224 | tf_op jit(solution)/shard_map/ppermute | solution.py:15
  250.1 8.6 %collective-permute-start.5 = (f32[1,256,128]{1,0,2:T(1,128)S(1)}, f32[1,256,128]{1,0,2:T(1,128)S(1)}, u32[]{:S(2)}, u32[]{:S(2)}) collective-permute-start(f32[1,256,128]{1,0,2:T(1,128)S(1)} %get-tuple-element.20), channel_id=1, source_target_pairs={{0,2},{2,4},{4,6},{6,8},{8,10},{10,12},{12,14},{14,16},{16,18},{18... | collective-permute-start | bytes 393224 | tf_op jit(solution)/shard_map/ppermute | solution.py:15
  264.1 6.4 %collective-permute-start.6 = (f32[1,256,128]{1,0,2:T(1,128)S(1)}, f32[1,256,128]{1,0,2:T(1,128)S(1)}, u32[]{:S(2)}, u32[]{:S(2)}) collective-permute-start(f32[1,256,128]{1,0,2:T(1,128)S(1)} %get-tuple-element.17), channel_id=1, source_target_pairs={{0,30},{2,0},{4,2},{6,4},{8,6},{10,8},{12,10},{14,12},{16,14},{18,... | collective-permute-start | bytes 393224 | tf_op jit(solution)/shard_map/ppermute | solution.py:15
  264.4 9.0 %collective-permute-start.7 = (f32[1,256,128]{1,0,2:T(1,128)S(1)}, f32[1,256,128]{1,0,2:T(1,128)S(1)}, u32[]{:S(2)}, u32[]{:S(2)}) collective-permute-start(f32[1,256,128]{1,0,2:T(1,128)S(1)} %get-tuple-element.18), channel_id=1, source_target_pairs={{0,2},{2,4},{4,6},{6,8},{8,10},{10,12},{12,14},{14,16},{16,18},{18... | collective-permute-start | bytes 393224 | tf_op jit(solution)/shard_map/ppermute | solution.py:15
where the time goes:
time: 316 us; the launch traced here: 314 us
  blocking collectives  242 us (77%)
  waiting for transfers between devices  27.8 us (9%)
  matrix products  13.8 us (4%)
  starting transfers between devices  12.2 us (4%)
  local copies, waits for them, and re-layouts  6.86 us (2%)
  between operations  5.8 us (2%)
  other arithmetic  5.78 us (2%)
    psum x2, blocking collectives, on_device(): coarse_in = lax.psum(partial_coarse(masked_dir), ('sub', 'face'))  80.1 us
    psum x2, blocking collectives, squares(): lax.psum(jnp.sum(entry_values * entry_values, axis=(0, 1)), ('sub', 'face'))  78 us
    psum x1, blocking collectives, on_device(): lax.psum((gram_part, partial_coarse(masked_loads)), ('sub', 'face'))  42.2 us
    psum x1, blocking collectives, on_device(): lax.psum((partial_coarse(folded), local_curv), ('sub', 'face'))  37 us
    ppermute x8, waiting for transfers between devices, passed_along(): return lax.ppermute(value, axis, pairs)  27.8 us
    ppermute x8, starting transfers between devices, passed_along(): return lax.ppermute(value, axis, pairs)  12.2 us
  transfers between devices with their start and end apart: 8, of which 7 were waited for; matrix products, arithmetic and copies ran while one was open for 0% of the time, Pallas kernels for 0%

commit v1 on v0

v1 whole, which is shorter than its diff:
```python
import functools

import jax
import jax.numpy as jnp
from jax import lax
from jax.experimental import pallas as pl
from jax.experimental.pallas import tpu as pltpu
from jax.sharding import PartitionSpec as P

MESH = pl.DeviceIdType.MESH
F32 = jnp.float32
BF16 = jnp.bfloat16
HIGHEST = lax.Precision.HIGHEST


def stage_plan(devices):
    plan = [(1, 2)]
    stride = 2
    while stride < devices:
        left = devices // stride
        radix = next(r for r in (4, 2, 3, 5, 7, left) if left % r == 0)
        plan.append((stride, radix))
        stride *= radix
    return plan


def kernel(
    subs,
    clusters,
    plan,
    schur_hbm,
    modes_ref,
    loads_ref,
    sizes_ref,
    contact_ref,
    friction_ref,
    cluster_ref,
    mult_ref,
    res_ref,
    s_buf,
    s_hi,
    s_lo,
    pack,
    pack_p,
    x_own,
    x_p,
    u_own,
    u_other,
    t_own,
    t_p,
    stacked,
    q_t,
    fr_t,
    mask_own,
    mask_sum,
    res0,
    res1,
    s_sem,
    ring_send,
    ring_recv,
    core_send,
    core_recv,
    red_send,
    red_recv,
    *slots,
):
    rows = loads_ref.shape[1]
    half = rows // 2
    cols = loads_ref.shape[2]
    n8 = 8 * clusters
    sub = lax.axis_index("sub")
    face = lax.axis_index("face")
    right = lax.rem(sub + 1, subs)
    left = lax.rem(sub + subs - 1, subs)
    linear = sub * 2 + face
    other = 1 - face

    peers = []
    for stride, radix in plan:
        digit = lax.rem(linear // stride, radix)
        group = []
        for k in range(1, radix):
            peer = linear + (lax.rem(digit + k, radix) - digit) * stride
            group.append((peer // 2, lax.rem(peer, 2)))
        peers.append((digit, group))

    barrier = pltpu.get_barrier_semaphore()
    total = 0
    for _, group in peers:
        for device in group:
            pl.semaphore_signal(barrier, inc=1, device_id=device, device_id_type=MESH)
            total += 1
    for device in ((right, face), (left, face)):
        pl.semaphore_signal(barrier, inc=1, device_id=device, device_id_type=MESH)
        total += 1

    other_cols = pl.multiple_of(other * rows, 128)
    own_cols = pl.multiple_of(face * rows, 128)
    s_copies = [
        pltpu.make_async_copy(schur_hbm.at[0, :, pl.ds(own_cols, rows)], s_buf.at[0], s_sem.at[0]),
        pltpu.make_async_copy(schur_hbm.at[0, :, pl.ds(other_cols, rows)], s_buf.at[1], s_sem.at[1]),
    ]
    for copy in s_copies:
        copy.start()

    sends = []

    def dot(a, b):
        return jnp.dot(a, b, preferred_element_type=F32, precision=HIGHEST)

    def ring(kind, src, dst, lanes):
        started = []
        for k, (device, lo, to) in enumerate(((right, 0, half), (left, half, 0))):
            if lanes:
                s_ref, d_ref = src.at[:, pl.ds(lo, half)], dst.at[:, pl.ds(to, half)]
            else:
                s_ref, d_ref = src.at[pl.ds(lo, half)], dst.at[pl.ds(to, half)]
            copy = pltpu.make_async_remote_copy(
                src_ref=s_ref,
                dst_ref=d_ref,
                send_sem=ring_send.at[2 * kind + k],
                recv_sem=ring_recv.at[2 * kind + k],
                device_id=(device, face),
                device_id_type=MESH,
            )
            copy.start()
            sends.append(copy)
            started.append(copy)
        return started

    def swap(index):
        copy = pltpu.make_async_remote_copy(
            src_ref=u_own.at[index],
            dst_ref=u_other.at[index],
            send_sem=core_send.at[index],
            recv_sem=core_recv.at[index],
            device_id=(sub, other),
            device_id_type=MESH,
        )
        copy.start()
        sends.append(copy)
        return copy

    per_red = sum(radix - 1 for _, radix in plan)

    def reduce_start(index, stage, store):
        ref = slots[index * len(plan) + stage]
        digit, group = peers[stage]
        store(ref, digit)
        base = index * per_red + sum(radix - 1 for _, radix in plan[:stage])
        copies = []
        for k, device in enumerate(group):
            copy = pltpu.make_async_remote_copy(
                src_ref=ref.at[digit],
                dst_ref=ref.at[digit],
                send_sem=red_send.at[base + k],
                recv_sem=red_recv.at[base + k],
                device_id=device,
                device_id_type=MESH,
            )
            copy.start()
            copies.append(copy)
            sends.append(copy)
        return ref, copies

    def reduce_end(started):
        ref, copies = started
        for copy in copies:
            copy.wait_recv()
        value = ref[0]
        for k in range(1, ref.shape[0]):
            value = value + ref[k]
        return value

    def put(value):
        def store(ref, digit):
            ref[digit] = value

        return store

    def all_reduce(index, store, meanwhile):
        started = reduce_start(index, 0, store)
        for stage in range(1, len(plan)):
            started = reduce_start(index, stage, put(reduce_end(started)))
        meanwhile()
        return reduce_end(started)

    position = lax.broadcasted_iota(jnp.int32, (1, half), 1)
    inside = jnp.concatenate(
        [
            jnp.where(position < sizes_ref[0, 0], 1.0, 0.0),
            jnp.where(position < sizes_ref[0, 1], 1.0, 0.0),
        ],
        axis=1,
    )
    blocked = (contact_ref[...] * (1 - friction_ref[...])).astype(F32)
    free = inside * (1.0 - blocked)
    pack[0:6, :] = modes_ref[0]
    pack[6:7, :] = jnp.full((1, rows), cluster_ref[0], jnp.int32).astype(F32)
    pack[7:8, :] = free

    def expand(ref):
        value = ref[...]
        row = lax.broadcasted_iota(jnp.int32, value.shape, 0)
        modes = jnp.where(row < 6, value, 0.0)
        ids = value[6:7, :]
        mask = value[7:8, :]
        per_cluster = jnp.concatenate(
            [jnp.where(ids == float(b), modes, 0.0) for b in range(clusters)], axis=0
        )
        return modes, per_cluster, per_cluster * mask, mask

    modes, rc, frc, mask = expand(pack)
    mask_own[...] = jnp.broadcast_to(mask, (128, rows)).T
    x_own[...] = loads_ref[0] * mask_own[...]
    stacked[...] = jnp.zeros_like(stacked)
    stacked[0:8, :] = modes
    stacked[8:16, :] = modes * mask
    gram_part = lax.dot_general(
        rc, stacked[...], (((1,), (1,)), ((), ())), preferred_element_type=F32, precision=HIGHEST
    )
    coarse_part = dot(rc, x_own[...])

    pl.semaphore_wait(barrier, total)

    def first_store(ref, digit):
        ref[digit, 0:n8, :] = coarse_part
        ref[digit, n8 : 2 * n8, :] = gram_part

    q = []

    def prepare():
        for k in range(2):
            s_copies[k].wait()
            value = s_buf[k]
            high = value.astype(BF16)
            s_hi[k] = high
            s_lo[k] = (value - high.astype(F32)).astype(BF16)
        for copy in pack_copies:
            copy.wait_recv()
        _, rc_p, frc_p, mask_p = expand(pack_p)
        both = jnp.concatenate([frc + frc_p, rc + rc_p], axis=0)
        q.append(both)
        q_t[...] = both.T
        fr_t[...] = frc.T
        mask_sum[...] = jnp.broadcast_to(mask + mask_p, (128, rows)).T
        for copy in x_copies:
            copy.wait_recv()

    started = reduce_start(0, 0, first_store)
    pack_copies = ring(0, pack, pack_p, True)
    x_copies = ring(1, x_own, x_p, False)
    for stage in range(1, len(plan)):
        started = reduce_start(0, stage, put(reduce_end(started)))
    prepare()
    first = reduce_end(started)
    q = q[0]

    shape3 = (clusters, 8, cols)
    coarse0 = first[0:n8].reshape(shape3)
    grams = first[n8 : 2 * n8].reshape(shape3)
    lane = lax.broadcasted_iota(jnp.int32, shape3, 2)
    row3 = lax.broadcasted_iota(jnp.int32, shape3, 1)
    work = (
        jnp.where(lane < 8, grams, 0.0)
        + jnp.where((lane == row3) & (row3 >= 6), 1.0, 0.0)
        + jnp.where(lane == row3 + 16, 1.0, 0.0)
    )
    for k in range(6):
        pivot_row = work[:, k : k + 1, :]
        pivot_row = pivot_row / pivot_row[:, :, k : k + 1]
        work = jnp.where(row3 == k, pivot_row, work - work[:, :, k : k + 1] * pivot_row)
    inv_cols = [jnp.broadcast_to(work[:, :, 16 + m : 17 + m], shape3) for m in range(6)]
    gf_cols = [jnp.broadcast_to(grams[:, :, 8 + m : 9 + m], shape3) for m in range(6)]

    def apply(columns, value):
        result = columns[0] * value[:, 0:1, :]
        for m in range(1, 6):
            result = result + columns[m] * value[:, m : m + 1, :]
        return result

    def flat(value):
        return value.reshape(n8, cols)

    def multiply(index, values):
        u_own[index, 0:half] = values[0:half]
        u_own[index, half:rows] = -values[half:rows]
        copy = swap(index)

        def part(k, value):
            high = value.astype(BF16)
            low = (value - high.astype(F32)).astype(BF16)
            wide = jnp.dot(
                s_hi[k], jnp.concatenate([high, low], axis=1), preferred_element_type=F32
            )
            narrow = jnp.dot(s_lo[k], high, preferred_element_type=F32)
            return wide[:, :cols] + wide[:, cols:] + narrow

        own = part(0, u_own[index])
        copy.wait_recv()
        image = own + part(1, u_other[index])
        t_own[index, 0:half] = image[0:half]
        t_own[index, half:rows] = -image[half:rows]

    def folded(index):
        return t_own[index] + t_p[index]

    def signed_u(index):
        return jnp.concatenate([u_own[index, 0:half], -u_own[index, half:rows]], axis=0)

    def sum_rows(value):
        return jnp.sum(value, axis=0, keepdims=True)

    c0 = apply(inv_cols, coarse0)
    coarse1 = coarse0 - apply(gf_cols, c0)
    w1 = apply(inv_cols, coarse1)
    x_both = x_own[...] + x_p[...]
    multiply(0, x_both - dot(q_t[...], jnp.concatenate([flat(c0), flat(w1)], axis=0)))
    t0_copies = ring(2, t_own.at[0], t_p.at[0], False)
    res0[...] = x_own[...] - dot(fr_t[...], flat(c0))

    def second_store(ref, digit):
        ref[digit, 0 : 2 * n8, :] = dot(q, t_own[0])
        ref[digit, 2 * n8 : 2 * n8 + 8, :] = jnp.zeros((8, cols), F32)
        ref[digit, 2 * n8 : 2 * n8 + 1, :] = sum_rows(signed_u(0) * t_own[0])
        ref[digit, 2 * n8 + 1 : 2 * n8 + 2, :] = sum_rows(res0[...] * res0[...])

    def wait_t0():
        for copy in t0_copies:
            copy.wait_recv()

    second = all_reduce(1, second_store, wait_t0)
    f_coarse = second[0:n8].reshape(shape3)
    r_coarse = second[n8 : 2 * n8].reshape(shape3)
    curvature0 = second[2 * n8 : 2 * n8 + 1]
    norm0 = second[2 * n8 + 1 : 2 * n8 + 2]
    step0 = norm0 / curvature0
    step_w = apply(inv_cols, r_coarse) * step0[None]
    coarse2 = coarse1 - step0[None] * f_coarse + apply(gf_cols, step_w)
    w2 = apply(inv_cols, coarse2)

    multiply(
        1,
        x_own[...]
        + x_p[...]
        - step0 * (mask_sum[...] * folded(0))
        - dot(q_t[...], jnp.concatenate([flat(c0 - step_w), flat(w2)], axis=0)),
    )
    t1_copies = ring(3, t_own.at[1], t_p.at[1], False)
    res1[...] = res0[...] - step0 * (mask_own[...] * folded(0)) + dot(fr_t[...], flat(step_w))

    def third_store(ref, digit):
        ref[digit, 0:n8, :] = dot(q[n8 : 2 * n8], t_own[1])
        ref[digit, n8 : n8 + 8, :] = jnp.zeros((8, cols), F32)
        ref[digit, n8 : n8 + 1, :] = sum_rows(signed_u(1) * t_own[1])
        ref[digit, n8 + 1 : n8 + 2, :] = sum_rows(signed_u(1) * t_own[0])
        ref[digit, n8 + 2 : n8 + 3, :] = sum_rows(res1[...] * res1[...])

    def wait_t1():
        for copy in t1_copies:
            copy.wait_recv()

    third = all_reduce(2, third_store, wait_t1)
    norm1 = third[n8 + 2 : n8 + 3]
    ratio = norm1 / norm0
    curvature1 = (
        third[n8 : n8 + 1] + ratio * (2.0 * third[n8 + 1 : n8 + 2]) + ratio * (ratio * curvature0)
    )
    step1 = norm1 / curvature1
    w_out = apply(inv_cols, third[0:n8].reshape(shape3) + ratio[None] * r_coarse) * step1[None]
    mult_ref[0] = step0 * res0[...] + step1 * (res1[...] + ratio * res0[...])
    res_ref[0] = (
        res1[...]
        - step1 * (mask_own[...] * (folded(1) + ratio * folded(0)))
        + dot(fr_t[...], flat(w_out))
    )
    for copy in sends:
        copy.wait_send()


def solution(mesh):
    subs = mesh.shape["sub"]
    devices = subs * mesh.shape["face"]
    plan = stage_plan(devices)

    def on_device(schur, modes, loads, sizes, contact, friction, cluster_ids, pairing):
        del pairing
        _, rows, cols = loads.shape
        clusters = subs // 8
        n8 = 8 * clusters
        vmem = pl.BlockSpec(memory_space=pltpu.VMEM)
        smem = pl.BlockSpec(memory_space=pltpu.SMEM)
        field = pltpu.VMEM((rows, cols), F32)
        pair = pltpu.VMEM((2, rows, cols), F32)
        slot_rows = (2 * n8, 2 * n8 + 8, n8 + 8)
        slots = [pltpu.VMEM((radix, count, cols), F32) for count in slot_rows for _, radix in plan]
        reds = 3 * sum(radix - 1 for _, radix in plan)
        return pl.pallas_call(
            functools.partial(kernel, subs, clusters, plan),
            out_shape=[jax.ShapeDtypeStruct(loads.shape, F32)] * 2,
            in_specs=[pl.BlockSpec(memory_space=pl.ANY), vmem, vmem, smem, vmem, vmem, smem],
            out_specs=[vmem, vmem],
            scratch_shapes=[
                pltpu.VMEM((2, rows, rows), F32),
                pltpu.VMEM((2, rows, rows), BF16),
                pltpu.VMEM((2, rows, rows), BF16),
                pltpu.VMEM((8, rows), F32),
                pltpu.VMEM((8, rows), F32),
                field,
                field,
                pair,
                pair,
                pair,
                pair,
                pltpu.VMEM((128, rows), F32),
                pltpu.VMEM((rows, 2 * n8), F32),
                pltpu.VMEM((rows, n8), F32),
                field,
                field,
                field,
                field,
                pltpu.SemaphoreType.DMA((2,)),
                pltpu.SemaphoreType.DMA((8,)),
                pltpu.SemaphoreType.DMA((8,)),
                pltpu.SemaphoreType.DMA((2,)),
                pltpu.SemaphoreType.DMA((2,)),
                pltpu.SemaphoreType.DMA((reds,)),
                pltpu.SemaphoreType.DMA((reds,)),
                *slots,
            ],
            compiler_params=pltpu.CompilerParams(
                collective_id=0, has_side_effects=True, vmem_limit_bytes=48 * 1024 * 1024
            ),
        )(schur, modes, loads, sizes, contact, friction, cluster_ids)

    placed = (
        P("sub", "face", None),
        P("sub", None, "face"),
        P("sub", "face", None),
        P("sub", "face"),
        P("sub", "face"),
        P("sub", "face"),
        P("sub"),
        P("sub", "face", None, None),
    )
    return jax.shard_map(
        on_device,
        mesh=mesh,
        in_specs=placed,
        out_specs=(P("sub", "face", None), P("sub", "face", None)),
        check_vma=False,
    )
```

time: 316 us -> 56.8 us (0.18)
  blocking collectives: 242 us -> 0 us
  Pallas kernels: 0 us -> 48.6 us
  waiting for transfers between devices: 27.8 us -> 0 us
  matrix products: 13.8 us -> 0 us
  starting transfers between devices: 12.2 us -> 0 us
  other arithmetic: 5.78 us -> 0 us
  between operations: 5.8 us -> 1.29 us
    psum x6 -> x0, blocking collectives: 237 us -> none  [the longest x2 80.1 us: on_device(): coarse_in = lax.psum(partial_coarse(masked_dir), ('sub', 'face'))]
    pallas_call x0 -> x1, Pallas kernels: none -> 48.6 us  [on_device(): pl.pallas_call(functools.partial(kernel, subs, clusters, plan), out_shape...]
    ppermute x8 -> x0, waiting for transfers between devices: 27.8 us -> none  [passed_along(): return lax.ppermute(value, axis, pairs)]
    dot_general x24 -> x0, matrix products: 13.6 us -> none  [the longest x2 4.48 us: on_device(): jnp.einsum('gkc,gcr->gkr', schur_blocks, lax.all_gather(joined, 'face', a...]
    ppermute x8 -> x0, starting transfers between devices: 12.2 us -> none  [passed_along(): return lax.ppermute(value, axis, pairs)]
    all_gather x2 -> x0, blocking collectives: 4.36 us -> none  [on_device(): lax.all_gather(joined, 'face', axis=1, tiled=True)]
    another operation x12 -> x0, other arithmetic: 3.21 us -> none  [the longest x4 1.24 us: coarse_inverse(): lower_factor = jnp.linalg.cholesky(coarse_gram)]
    unnamed x15 -> x13, local copies, waits for them, and re-layouts: 3.56 us -> 6.67 us
  transfers between devices with their start and end apart: 8 -> 0, of which waited for: 7 -> 0; matrix products, arithmetic and copies ran while one was open for 0% -> 0% of each run, Pallas kernels for 0% -> 0%
where the time goes in v1:
time: 56.8 us; the launch traced here: 56.5 us
  Pallas kernels  48.6 us (86%)
  local copies, waits for them, and re-layouts  6.67 us (12%)
  between operations  1.29 us (2%)
    pallas_call x1, Pallas kernels, on_device(): pl.pallas_call(functools.partial(kernel, subs, clusters, plan), out_shape...  48.6 us
    unnamed x13, local copies, waits for them, and re-layouts  6.67 us

profile of v1, /device:TPU:0, one launch (start us, length us, event | category | flops | bytes accessed | tf_op | source)
XLA Modules:
  0.0 56.5 jit_solution(17832358325011503371)
XLA Ops:
  1.3 0.7 %copy.9.modes_ref = f32[1,6,512]{2,1,0:T(8,128)S(1)} copy(f32[1,6,512]{2,0,1:T(1,128)} %param.9) | data formatting | bytes 24576 | tf_op args[1]
  2.0 0.0 copy-start
  2.0 1.6 %copy-done = f32[1,512,1024]{2,1,0:T(8,128)S(1)} copy-done((f32[1,512,1024]{2,1,0:T(8,128)S(1)}, f32[1,512,1024]{2,1,0:T(8,128)}, u32[]{:S(2)}) %copy-start) | copy-done | bytes 2097176
  3.6 0.0 copy-start.1
  3.6 0.9 %copy-done.1 = f32[1,512,128]{2,1,0:T(8,128)S(1)} copy-done((f32[1,512,128]{2,1,0:T(8,128)S(1)}, f32[1,512,128]{2,1,0:T(8,128)}, u32[]{:S(2)}) %copy-start.1) | copy-done | bytes 262168
  4.5 0.0 copy-start.2
  4.5 0.7 %copy-done.2 = s32[1,512]{1,0:T(1,128)S(1)} copy-done((s32[1,512]{1,0:T(1,128)S(1)}, s32[1,512]{1,0:T(1,128)}, u32[]{:S(2)}) %copy-start.2) | copy-done | bytes 2072
  5.2 0.0 copy-start.3
  5.2 0.7 %copy-done.3 = s32[1,512]{1,0:T(1,128)S(1)} copy-done((s32[1,512]{1,0:T(1,128)S(1)}, s32[1,512]{1,0:T(1,128)}, u32[]{:S(2)}) %copy-start.3) | copy-done | bytes 2072
  5.9 0.0 copy-start.4
  5.9 0.7 %copy-done.4 = s32[1,2]{1,0:T(1,128)S(1)} copy-done((s32[1,2]{1,0:T(1,128)S(1)}, s32[1,2]{1,0:T(1,128)}, u32[]{:S(2)}) %copy-start.4) | copy-done | bytes 32
  6.5 48.6 %shard_map.86 = (f32[1,512,128]{2,1,0:T(8,128)S(1)}, f32[1,512,128]{2,1,0:T(8,128)S(1)}) custom-call(f32[1,512,1024]{2,1,0:T(8,128)S(1)} %copy-done, f32[1,6,512]{2,1,0:T(8,128)S(1)} %copy.9.modes_ref, f32[1,512,128]{2,1,0:T(8,128)S(1)} %copy-done.1, s32[1,2]{1,0:T(1,128)S(1)} %copy-done.4, s32[1,512]{1,0:T(1,128)S(1)} %copy-done.2, s32[1,512]{1,0:T(1,128)S(1)} %copy-done.3, ...), custom_call_target="tpu_custom_call" | custom-call | tf_op jit(solution)/shard_map/pallas_call | solution.py:398
  55.1 0.7 %copy.13 = f32[1,512,128]{2,1,0:T(8,128)} copy(f32[1,512,128]{2,1,0:T(8,128)S(1)} %get-tuple-element.4) | data formatting | bytes 524288
  55.8 0.7 %copy.14 = f32[1,512,128]{2,1,0:T(8,128)} copy(f32[1,512,128]{2,1,0:T(8,128)S(1)} %get-tuple-element.5) | data formatting | bytes 524288
Async XLA Ops:
  2.0 1.6 %copy-start = (f32[1,512,1024]{2,1,0:T(8,128)S(1)}, f32[1,512,1024]{2,1,0:T(8,128)}, u32[]{:S(2)}) copy-start(f32[1,512,1024]{2,1,0:T(8,128)} %schur_hbm.1) | copy-start | bytes 6291460
  3.6 0.9 %copy-start.1 = (f32[1,512,128]{2,1,0:T(8,128)S(1)}, f32[1,512,128]{2,1,0:T(8,128)}, u32[]{:S(2)}) copy-start(f32[1,512,128]{2,1,0:T(8,128)} %loads_ref.1) | copy-start | bytes 786436
  4.5 0.7 %copy-start.2 = (s32[1,512]{1,0:T(1,128)S(1)}, s32[1,512]{1,0:T(1,128)}, u32[]{:S(2)}) copy-start(s32[1,512]{1,0:T(1,128)} %contact_ref.1) | copy-start | bytes 6148
  5.2 0.7 %copy-start.3 = (s32[1,512]{1,0:T(1,128)S(1)}, s32[1,512]{1,0:T(1,128)}, u32[]{:S(2)}) copy-start(s32[1,512]{1,0:T(1,128)} %friction_ref.1) | copy-start | bytes 6148
  5.9 0.7 %copy-start.4 = (s32[1,2]{1,0:T(1,128)S(1)}, s32[1,2]{1,0:T(1,128)}, u32[]{:S(2)}) copy-start(s32[1,2]{1,0:T(1,128)} %sizes_ref.1) | copy-start | bytes 28

commit v2 on v1

v2 whole, which is shorter than its diff:
```python
import functools

import jax
import jax.numpy as jnp
from jax import lax
from jax.experimental import pallas as pl
from jax.experimental.pallas import tpu as pltpu
from jax.sharding import PartitionSpec as P

MESH = pl.DeviceIdType.MESH
F32 = jnp.float32
BF16 = jnp.bfloat16
HIGHEST = lax.Precision.HIGHEST


def stage_plan(devices):
    plan = []
    stride = 2
    while stride < devices:
        left = devices // stride
        radix = next(r for r in (4, 2, 3, 5, 7, left) if left % r == 0)
        plan.append((stride, radix))
        stride *= radix
    return [(1, 2)] + plan[::-1]


def kernel(
    subs,
    clusters,
    plan,
    schur_hbm,
    modes_hbm,
    loads_hbm,
    sizes_hbm,
    contact_hbm,
    friction_hbm,
    cluster_hbm,
    mult_ref,
    res_ref,
    s_buf,
    loads_buf,
    modes_buf,
    contact_buf,
    friction_buf,
    sizes_buf,
    cluster_buf,
    s_hi,
    s_lo,
    pack,
    pack_p,
    q_own,
    q_other,
    x_own,
    x_p,
    v_own,
    v_other,
    y_own,
    y_p,
    stacked,
    low_image,
    low_u,
    low_res,
    mask_own,
    mask_sum,
    image,
    u_now,
    res0,
    res1,
    in_sem,
    ring_send,
    ring_recv,
    core_send,
    core_recv,
    red_send,
    red_recv,
    *slots,
):
    rows, cols = loads_buf.shape
    half = rows // 2
    n8 = 8 * clusters
    sub = lax.axis_index("sub")
    face = lax.axis_index("face")
    right = lax.rem(sub + 1, subs)
    left = lax.rem(sub + subs - 1, subs)
    linear = sub * 2 + face
    other = 1 - face

    own_cols = pl.multiple_of(face * rows, 128)
    other_cols = pl.multiple_of(other * rows, 128)
    inputs = [
        pltpu.make_async_copy(src, dst, in_sem.at[k])
        for k, (src, dst) in enumerate(
            (
                (sizes_hbm, sizes_buf),
                (cluster_hbm, cluster_buf),
                (contact_hbm, contact_buf),
                (friction_hbm, friction_buf),
                (modes_hbm, modes_buf),
                (loads_hbm.at[0], loads_buf),
                (schur_hbm.at[0, :, pl.ds(own_cols, rows)], s_buf.at[0]),
                (schur_hbm.at[0, :, pl.ds(other_cols, rows)], s_buf.at[1]),
            )
        )
    ]
    for copy in inputs:
        copy.start()

    peers = []
    for stride, radix in plan:
        digit = lax.rem(linear // stride, radix)
        group = []
        for k in range(1, radix):
            peer = linear + (lax.rem(digit + k, radix) - digit) * stride
            group.append((peer // 2, lax.rem(peer, 2)))
        peers.append((digit, group))

    barrier = pltpu.get_barrier_semaphore()
    total = 0
    for _, group in peers:
        for device in group:
            pl.semaphore_signal(barrier, inc=1, device_id=device, device_id_type=MESH)
            total += 1
    for device in ((right, face), (left, face)):
        pl.semaphore_signal(barrier, inc=1, device_id=device, device_id_type=MESH)
        total += 1

    sends = []

    def dot(a, b):
        return jnp.dot(a, b, preferred_element_type=F32, precision=HIGHEST)

    def ring(kind, src, dst, lanes):
        started = []
        for k, (device, lo, to) in enumerate(((right, 0, half), (left, half, 0))):
            if lanes:
                s_ref, d_ref = src.at[:, pl.ds(lo, half)], dst.at[:, pl.ds(to, half)]
            else:
                s_ref, d_ref = src.at[pl.ds(lo, half)], dst.at[pl.ds(to, half)]
            copy = pltpu.make_async_remote_copy(
                src_ref=s_ref,
                dst_ref=d_ref,
                send_sem=ring_send.at[2 * kind + k],
                recv_sem=ring_recv.at[2 * kind + k],
                device_id=(device, face),
                device_id_type=MESH,
            )
            copy.start()
            sends.append(copy)
            started.append(copy)
        return started

    def swap(index, src, dst):
        copy = pltpu.make_async_remote_copy(
            src_ref=src,
            dst_ref=dst,
            send_sem=core_send.at[index],
            recv_sem=core_recv.at[index],
            device_id=(sub, other),
            device_id_type=MESH,
        )
        copy.start()
        sends.append(copy)
        return copy

    per_red = sum(radix - 1 for _, radix in plan)

    def reduce_start(index, stage, store):
        ref = slots[index * len(plan) + stage]
        digit, group = peers[stage]
        store(ref, digit)
        base = index * per_red + sum(radix - 1 for _, radix in plan[:stage])
        copies = []
        for k, device in enumerate(group):
            copy = pltpu.make_async_remote_copy(
                src_ref=ref.at[digit],
                dst_ref=ref.at[digit],
                send_sem=red_send.at[base + k],
                recv_sem=red_recv.at[base + k],
                device_id=device,
                device_id_type=MESH,
            )
            copy.start()
            copies.append(copy)
            sends.append(copy)
        return ref, copies

    def reduce_end(started):
        ref, copies = started
        for copy in copies:
            copy.wait_recv()
        value = ref[0]
        for k in range(1, ref.shape[0]):
            value = value + ref[k]
        return value

    def put(value):
        def store(ref, digit):
            ref[digit] = value

        return store

    def all_reduce(index, store, meanwhile):
        started = reduce_start(index, 0, store)
        for stage in range(1, len(plan)):
            if stage - 1 < len(meanwhile) - 1:
                meanwhile[stage - 1]()
            started = reduce_start(index, stage, put(reduce_end(started)))
        meanwhile[-1]()
        return reduce_end(started)

    def split3(value):
        first = value.astype(BF16)
        rest = value - first.astype(F32)
        second = rest.astype(BF16)
        third = (rest - second.astype(F32)).astype(BF16)
        return first, second, third

    def low_left(value):
        a, b, c = split3(value)
        return jnp.concatenate([a, a, a, b, b, c], axis=1)

    def low_right(value):
        a, b, c = split3(value)
        return jnp.concatenate([a, b, c, a, b, a], axis=0)

    def bdot(a, b):
        return jnp.dot(a, b, preferred_element_type=F32)

    for copy in inputs[:5]:
        copy.wait()
    position = lax.broadcasted_iota(jnp.int32, (1, half), 1)
    inside = jnp.concatenate(
        [
            jnp.where(position < sizes_buf[0, 0], 1.0, 0.0),
            jnp.where(position < sizes_buf[0, 1], 1.0, 0.0),
        ],
        axis=1,
    )
    blocked = (contact_buf[...] * (1 - friction_buf[...])).astype(F32)
    free = inside * (1.0 - blocked)
    for m in range(6):
        pack[m : m + 1, :] = modes_buf[m]
    pack[6:7, :] = jnp.full((1, rows), cluster_buf[0], jnp.int32).astype(F32)
    pack[7:8, :] = free

    def expand(ref):
        value = ref[...]
        row = lax.broadcasted_iota(jnp.int32, value.shape, 0)
        modes = jnp.where(row < 6, value, 0.0)
        ids = value[6:7, :]
        mask = value[7:8, :]
        per_cluster = jnp.concatenate(
            [jnp.where(ids == float(b), modes, 0.0) for b in range(clusters)], axis=0
        )
        return modes, per_cluster, per_cluster * mask, mask

    modes, rc, frc, mask = expand(pack)
    lane_sign = jnp.where(lax.broadcasted_iota(jnp.int32, (1, rows), 1) < half, 1.0, -1.0)
    mask_wide = jnp.broadcast_to(mask, (128, rows)).T
    inputs[5].wait()
    x_own[...] = loads_buf[...] * mask_wide
    pl.semaphore_wait(barrier, total)
    pack_copies = ring(0, pack, pack_p, True)
    x_copies = ring(1, x_own, x_p, False)

    stacked[...] = jnp.zeros_like(stacked)
    stacked[0:8, :] = modes
    stacked[8:16, :] = modes * mask

    def first_store(ref, digit):
        ref[digit, 0:n8, :] = dot(rc, x_own[...])
        ref[digit, n8 : 2 * n8, :] = lax.dot_general(
            rc, stacked[...], (((1,), (1,)), ((), ())), preferred_element_type=F32, precision=HIGHEST
        )

    def split_schur():
        mask_own[0:half] = mask_wide[0:half]
        mask_own[half:rows] = -mask_wide[half:rows]
        for k in range(2):
            inputs[6 + k].wait()
            value = s_buf[k]
            high = value.astype(BF16)
            s_hi[k, 0:rows] = high
            s_lo[k, 0:rows] = (value - high.astype(F32)).astype(BF16)

    def product(value_own, fetch_other):
        def part(k, value):
            high = value.astype(BF16)
            low = (value - high.astype(F32)).astype(BF16)
            wide = bdot(s_hi[k], jnp.concatenate([high, low], axis=1))
            return wide[:, :cols] + wide[:, cols:] + bdot(s_lo[k], high)

        own = part(0, value_own)
        return own + part(1, fetch_other())

    swapped = []

    def fold_modes():
        for copy in pack_copies:
            copy.wait_recv()
        _, rc_p, frc_p, mask_p = expand(pack_p)
        q_own[...] = jnp.concatenate([frc + frc_p, rc + rc_p], axis=0) * lane_sign
        swapped.append(swap(0, q_own, q_other))
        mask_sum[...] = jnp.broadcast_to(mask + mask_p, (128, rows)).T
        split_schur()

    def swap_product(index):
        copy = swap(1 + index, v_own.at[index], v_other.at[index])

        def fetch():
            copy.wait_recv()
            return v_other[index]

        return product(v_own[index], fetch)

    def first_product():
        q = q_own[...]
        q_high = q.astype(BF16)
        q_low = (q - q_high.astype(F32)).astype(BF16)
        for k in range(2):
            wide = bdot(jnp.concatenate([q_high, q_low], axis=0), s_hi[k, 0:rows])
            coarse = wide[0 : 2 * n8] + wide[2 * n8 :] + bdot(q_high, s_lo[k, 0:rows])
            high = coarse.astype(BF16)
            s_hi[k, rows : rows + 2 * n8] = high
            s_lo[k, rows : rows + 2 * n8] = (coarse - high.astype(F32)).astype(BF16)
        q_t = q.T
        low_u[...] = low_left(q_t)
        low_res[...] = low_left(
            jnp.concatenate([frc.T, jnp.zeros((rows, n8), F32)], axis=1)
        )
        swapped[0].wait_recv()
        total_image = jnp.zeros((rows + 2 * n8, 2 * n8), F32)
        for k, value in enumerate((q_t, q_other[...].T)):
            high = value.astype(BF16)
            low = (value - high.astype(F32)).astype(BF16)
            total_image += bdot(s_hi[k], high) + bdot(s_hi[k], low) + bdot(s_lo[k], high)
        low_image[...] = low_left(total_image)
        for copy in x_copies:
            copy.wait_recv()
        both = x_own[...] + x_p[...]
        v_own[0, 0:half] = both[0:half]
        v_own[0, half:rows] = -both[half:rows]
        image[...] = swap_product(0)

    first = all_reduce(0, first_store, [fold_modes, first_product])

    shape3 = (clusters, 8, cols)
    coarse0 = first[0:n8].reshape(shape3)
    grams = first[n8 : 2 * n8].reshape(shape3)
    lane = lax.broadcasted_iota(jnp.int32, shape3, 2)
    row3 = lax.broadcasted_iota(jnp.int32, shape3, 1)
    work = (
        jnp.where(lane < 8, grams, 0.0)
        + jnp.where((lane == row3) & (row3 >= 6), 1.0, 0.0)
        + jnp.where(lane == row3 + 16, 1.0, 0.0)
    )
    for k in range(6):
        pivot_row = work[:, k : k + 1, :]
        pivot_row = pivot_row / pivot_row[:, :, k : k + 1]
        work = jnp.where(row3 == k, pivot_row, work - work[:, :, k : k + 1] * pivot_row)
    inv_cols = [jnp.broadcast_to(work[:, :, 16 + m : 17 + m], shape3) for m in range(6)]
    gf_cols = [jnp.broadcast_to(grams[:, :, 8 + m : 9 + m], shape3) for m in range(6)]

    def apply(columns, value):
        result = columns[0] * value[:, 0:1, :]
        for m in range(1, 6):
            result = result + columns[m] * value[:, m : m + 1, :]
        return result

    def flat(value):
        return value.reshape(n8, cols)

    def pair(a, b):
        return low_right(jnp.concatenate([flat(a), flat(b)], axis=0))

    def sum_rows(value):
        return jnp.sum(value, axis=0, keepdims=True)

    c0 = apply(inv_cols, coarse0)
    coarse1 = coarse0 - apply(gf_cols, c0)
    w1 = apply(inv_cols, coarse1)
    weights0 = pair(c0, w1)
    now = image[...] - bdot(low_image[...], weights0)
    y_own[0] = now[0:rows]
    y0_copies = ring(2, y_own.at[0], y_p.at[0], False)
    coarse_rows0 = now[rows:]
    image[rows:] = coarse_rows0

    def second_store(ref, digit):
        u_now[...] = v_own[0] - bdot(low_u[...], weights0)
        res0[...] = x_own[...] - bdot(low_res[...], weights0)
        ref[digit, 0 : 2 * n8, :] = coarse_rows0
        ref[digit, 2 * n8 : 2 * n8 + 8, :] = jnp.zeros((8, cols), F32)
        ref[digit, 2 * n8 : 2 * n8 + 1, :] = sum_rows(u_now[...] * y_own[0])
        ref[digit, 2 * n8 + 1 : 2 * n8 + 2, :] = sum_rows(res0[...] * res0[...])

    second_image = []

    def second_product():
        for copy in y0_copies:
            copy.wait_recv()
        v_own[1] = mask_sum[...] * (y_own[0] - y_p[0])
        second_image.append(swap_product(1))

    second = all_reduce(1, second_store, [second_product])
    f_coarse = second[0:n8].reshape(shape3)
    r_coarse = second[n8 : 2 * n8].reshape(shape3)
    curvature0 = second[2 * n8 : 2 * n8 + 1]
    norm0 = second[2 * n8 + 1 : 2 * n8 + 2]
    step0 = norm0 / curvature0
    step_w = apply(inv_cols, r_coarse) * step0[None]
    coarse2 = coarse1 - step0[None] * f_coarse + apply(gf_cols, step_w)
    w2 = apply(inv_cols, coarse2)

    weights1 = pair(step_w, w1 - w2)
    change = second_image[0] * step0 - bdot(low_image[...], weights1)
    y_own[1] = y_own[0] - change[0:rows]
    y1_copies = ring(3, y_own.at[1], y_p.at[1], False)

    def third_store(ref, digit):
        u_next = u_now[...] - step0 * v_own[1] + bdot(low_u[...], weights1)
        res1[...] = (
            res0[...]
            - step0 * (mask_own[...] * (y_own[0] - y_p[0]))
            + bdot(low_res[...], weights1)
        )
        ref[digit, 0:n8, :] = image[rows + n8 :] - change[rows + n8 :]
        ref[digit, n8 : n8 + 8, :] = jnp.zeros((8, cols), F32)
        ref[digit, n8 : n8 + 1, :] = sum_rows(u_next * y_own[1])
        ref[digit, n8 + 1 : n8 + 2, :] = sum_rows(u_next * y_own[0])
        ref[digit, n8 + 2 : n8 + 3, :] = sum_rows(res1[...] * res1[...])

    def wait_y1():
        for copy in y1_copies:
            copy.wait_recv()

    third = all_reduce(2, third_store, [wait_y1])
    norm1 = third[n8 + 2 : n8 + 3]
    ratio = norm1 / norm0
    curvature1 = (
        third[n8 : n8 + 1] + ratio * (2.0 * third[n8 + 1 : n8 + 2]) + ratio * (ratio * curvature0)
    )
    step1 = norm1 / curvature1
    w_out = apply(inv_cols, third[0:n8].reshape(shape3) + ratio[None] * r_coarse) * step1[None]
    mult_ref[0] = step0 * res0[...] + step1 * (res1[...] + ratio * res0[...])
    jump = (y_own[1] - y_p[1]) + ratio * (y_own[0] - y_p[0])
    res_ref[0] = (
        res1[...]
        - step1 * (mask_own[...] * jump)
        + bdot(low_res[...], pair(w_out, jnp.zeros_like(w_out)))
    )
    for copy in sends:
        copy.wait_send()


def solution(mesh):
    subs = mesh.shape["sub"]
    devices = subs * mesh.shape["face"]
    plan = stage_plan(devices)

    def on_device(schur, modes, loads, sizes, contact, friction, cluster_ids, pairing):
        del pairing
        _, rows, cols = loads.shape
        clusters = subs // 8
        n8 = 8 * clusters
        vmem = pl.BlockSpec(memory_space=pltpu.VMEM)
        field = pltpu.VMEM((rows, cols), F32)
        pair = pltpu.VMEM((2, rows, cols), F32)
        slot_rows = (2 * n8, 2 * n8 + 8, n8 + 8)
        slots = [pltpu.VMEM((radix, count, cols), F32) for count in slot_rows for _, radix in plan]
        reds = 3 * sum(radix - 1 for _, radix in plan)
        anywhere = pl.BlockSpec(memory_space=pl.ANY)
        tall = rows + 2 * n8
        return pl.pallas_call(
            functools.partial(kernel, subs, clusters, plan),
            out_shape=[jax.ShapeDtypeStruct(loads.shape, F32)] * 2,
            in_specs=[anywhere] * 7,
            out_specs=[vmem, vmem],
            scratch_shapes=[
                pltpu.VMEM((2, rows, rows), F32),
                field,
                pltpu.VMEM((6, 1, rows), F32),
                pltpu.VMEM((1, rows), jnp.int32),
                pltpu.VMEM((1, rows), jnp.int32),
                pltpu.SMEM((1, 2), jnp.int32),
                pltpu.SMEM((1,), jnp.int32),
                pltpu.VMEM((2, tall, rows), BF16),
                pltpu.VMEM((2, tall, rows), BF16),
                pltpu.VMEM((8, rows), F32),
                pltpu.VMEM((8, rows), F32),
                pltpu.VMEM((2 * n8, rows), F32),
                pltpu.VMEM((2 * n8, rows), F32),
                field,
                field,
                pair,
                pair,
                pair,
                pair,
                pltpu.VMEM((128, rows), F32),
                pltpu.VMEM((tall, 12 * n8), BF16),
                pltpu.VMEM((rows, 12 * n8), BF16),
                pltpu.VMEM((rows, 12 * n8), BF16),
                field,
                field,
                pltpu.VMEM((tall, cols), F32),
                field,
                field,
                field,
                pltpu.SemaphoreType.DMA((8,)),
                pltpu.SemaphoreType.DMA((8,)),
                pltpu.SemaphoreType.DMA((8,)),
                pltpu.SemaphoreType.DMA((3,)),
                pltpu.SemaphoreType.DMA((3,)),
                pltpu.SemaphoreType.DMA((reds,)),
                pltpu.SemaphoreType.DMA((reds,)),
                *slots,
            ],
            compiler_params=pltpu.CompilerParams(
                collective_id=0, has_side_effects=True, vmem_limit_bytes=60 * 1024 * 1024
            ),
        )(
            schur,
            modes.reshape(modes.shape[1], 1, rows),
            loads,
            sizes,
            contact,
            friction,
            cluster_ids,
        )

    placed = (
        P("sub", "face", None),
        P("sub", None, "face"),
        P("sub", "face", None),
        P("sub", "face"),
        P("sub", "face"),
        P("sub", "face"),
        P("sub"),
        P("sub", "face", None, None),
    )
    return jax.shard_map(
        on_device,
        mesh=mesh,
        in_specs=placed,
        out_specs=(P("sub", "face", None), P("sub", "face", None)),
        check_vma=False,
    )
```

time: 56.8 us -> 46.8 us (0.82)
  Pallas kernels: 48.6 us -> 42 us
  local copies, waits for them, and re-layouts: 6.67 us -> 3.34 us
    pallas_call x1, Pallas kernels: 48.6 us -> 42 us  [on_device(): pl.pallas_call(functools.partial(kernel, subs, clusters, plan), out_shape...]
    unnamed x13 -> x2, local copies, waits for them, and re-layouts: 6.67 us -> 3.34 us
where the time goes in v2:
time: 46.8 us; the launch traced here: 46.6 us
  Pallas kernels  42 us (90%)
  local copies, waits for them, and re-layouts  3.34 us (7%)
  between operations  1.29 us (3%)
    pallas_call x1, Pallas kernels, on_device(): pl.pallas_call(functools.partial(kernel, subs, clusters, plan), out_shape...  42 us
    unnamed x2, local copies, waits for them, and re-layouts  3.34 us

profile of v2, /device:TPU:0, one launch (start us, length us, event | category | flops | bytes accessed | tf_op | source)
XLA Modules:
  0.0 46.6 jit_solution(17533557899967109450)
XLA Ops:
  1.3 42.0 %shard_map.86 = (f32[1,512,128]{2,1,0:T(8,128)}, f32[1,512,128]{2,1,0:T(8,128)}) custom-call(f32[1,512,1024]{2,1,0:T(8,128)} %schur_hbm.1, f32[6,1,512]{2,1,0:T(1,128)} %bitcast.1, f32[1,512,128]{2,1,0:T(8,128)} %loads_hbm.1, s32[1,2]{1,0:T(1,128)} %sizes_hbm.1, s32[1,512]{1,0:T(1,128)} %contact_hbm.1, s32[1,512]{1,0:T(1,128)} %friction_hbm.1, ...), custom_call_target="tpu_custom_call" | custom-call | tf_op jit(solution)/shard_map/pallas_call | solution.py:474
  43.2 1.7 %copy.12 = f32[1,512,128]{2,1,0:T(8,128)} copy(f32[1,512,128]{2,1,0:T(8,128)} %get-tuple-element.4) | data formatting | bytes 524288
  44.9 1.7 %copy.13 = f32[1,512,128]{2,1,0:T(8,128)} copy(f32[1,512,128]{2,1,0:T(8,128)} %get-tuple-element.5) | data formatting | bytes 524288

commit v3 on v2

--- a/solution.py
+++ b/solution.py
@@ -21,7 +21,7 @@
         radix = next(r for r in (4, 2, 3, 5, 7, left) if left % r == 0)
         plan.append((stride, radix))
         stride *= radix
-    return [(1, 2)] + plan[::-1]
+    return plan[:0:-1] + [(1, 2 * plan[0][1])]
 
 
 def kernel(
@@ -216,8 +216,16 @@
         return first, second, third
 
     def low_left(value):
-        a, b, c = split3(value)
-        return jnp.concatenate([a, a, a, b, b, c], axis=1)
+        count = value.shape[1]
+        row = lax.broadcasted_iota(jnp.int32, (count, 6 * count), 0)
+        col = lax.broadcasted_iota(jnp.int32, (count, 6 * count), 1)
+        total_spread = 0.0
+        for piece, (lo, hi) in zip(split3(value), ((0, 3), (3, 5), (5, 6))):
+            spread = jnp.zeros(row.shape, F32)
+            for k in range(lo, hi):
+                spread += jnp.where(col == row + k * count, 1.0, 0.0)
+            total_spread += bdot(piece, spread.astype(BF16))
+        return total_spread.astype(BF16)
 
     def low_right(value):
         a, b, c = split3(value)
@@ -390,9 +398,8 @@
         u_now[...] = v_own[0] - bdot(low_u[...], weights0)
         res0[...] = x_own[...] - bdot(low_res[...], weights0)
         ref[digit, 0 : 2 * n8, :] = coarse_rows0
-        ref[digit, 2 * n8 : 2 * n8 + 8, :] = jnp.zeros((8, cols), F32)
-        ref[digit, 2 * n8 : 2 * n8 + 1, :] = sum_rows(u_now[...] * y_own[0])
-        ref[digit, 2 * n8 + 1 : 2 * n8 + 2, :] = sum_rows(res0[...] * res0[...])
+        ref[digit, 6:7, :] = sum_rows(u_now[...] * y_own[0])
+        ref[digit, 7:8, :] = sum_rows(res0[...] * res0[...])
 
     second_image = []
 
@@ -405,8 +412,8 @@
     second = all_reduce(1, second_store, [second_product])
     f_coarse = second[0:n8].reshape(shape3)
     r_coarse = second[n8 : 2 * n8].reshape(shape3)
-    curvature0 = second[2 * n8 : 2 * n8 + 1]
-    norm0 = second[2 * n8 + 1 : 2 * n8 + 2]
+    curvature0 = second[6:7]
+    norm0 = second[7:8]
     step0 = norm0 / curvature0
     step_w = apply(inv_cols, r_coarse) * step0[None]
     coarse2 = coarse1 - step0[None] * f_coarse + apply(gf_cols, step_w)
@@ -425,20 +432,19 @@
             + bdot(low_res[...], weights1)
         )
         ref[digit, 0:n8, :] = image[rows + n8 :] - change[rows + n8 :]
-        ref[digit, n8 : n8 + 8, :] = jnp.zeros((8, cols), F32)
-        ref[digit, n8 : n8 + 1, :] = sum_rows(u_next * y_own[1])
-        ref[digit, n8 + 1 : n8 + 2, :] = sum_rows(u_next * y_own[0])
-        ref[digit, n8 + 2 : n8 + 3, :] = sum_rows(res1[...] * res1[...])
+        ref[digit, 6:7, :] = sum_rows(u_next * y_own[1])
+        ref[digit, 7:8, :] = sum_rows(u_next * y_own[0])
+        ref[digit, 14:15, :] = sum_rows(res1[...] * res1[...])
 
     def wait_y1():
         for copy in y1_copies:
             copy.wait_recv()
 
     third = all_reduce(2, third_store, [wait_y1])
-    norm1 = third[n8 + 2 : n8 + 3]
+    norm1 = third[14:15]
     ratio = norm1 / norm0
     curvature1 = (
-        third[n8 : n8 + 1] + ratio * (2.0 * third[n8 + 1 : n8 + 2]) + ratio * (ratio * curvature0)
+        third[6:7] + ratio * (2.0 * third[7:8]) + ratio * (ratio * curvature0)
     )
     step1 = norm1 / curvature1
     w_out = apply(inv_cols, third[0:n8].reshape(shape3) + ratio[None] * r_coarse) * step1[None]
@@ -466,15 +472,14 @@
         vmem = pl.BlockSpec(memory_space=pltpu.VMEM)
         field = pltpu.VMEM((rows, cols), F32)
         pair = pltpu.VMEM((2, rows, cols), F32)
-        slot_rows = (2 * n8, 2 * n8 + 8, n8 + 8)
+        slot_rows = (2 * n8, 2 * n8, n8)
         slots = [pltpu.VMEM((radix, count, cols), F32) for count in slot_rows for _, radix in plan]
         reds = 3 * sum(radix - 1 for _, radix in plan)
-        anywhere = pl.BlockSpec(memory_space=pl.ANY)
         tall = rows + 2 * n8
         return pl.pallas_call(
             functools.partial(kernel, subs, clusters, plan),
             out_shape=[jax.ShapeDtypeStruct(loads.shape, F32)] * 2,
-            in_specs=[anywhere] * 7,
+            in_specs=[pl.BlockSpec(memory_space=pl.ANY)] * 7,
             out_specs=[vmem, vmem],
             scratch_shapes=[
                 pltpu.VMEM((2, rows, rows), F32),

time: 46.8 us -> 45.3 us (0.968)
  Pallas kernels: 42 us -> 40.5 us
    pallas_call x1, Pallas kernels: 42 us -> 40.5 us  [on_device(): pl.pallas_call(functools.partial(kernel, subs, clusters, plan), out_shape...]
where the time goes in v3:
time: 45.3 us; the launch traced here: 45.1 us
  Pallas kernels  40.5 us (89%)
  local copies, waits for them, and re-layouts  3.34 us (7%)
  between operations  1.29 us (3%)
    pallas_call x1, Pallas kernels, on_device(): pl.pallas_call(functools.partial(kernel, subs, clusters, plan), out_shape...  40.5 us
    unnamed x2, local copies, waits for them, and re-layouts  3.34 us

profile of v3, /device:TPU:0, one launch (start us, length us, event | category | flops | bytes accessed | tf_op | source)
XLA Modules:
  0.0 45.1 jit_solution(9319625005244781422)
XLA Ops:
  1.3 40.5 %shard_map.86 = (f32[1,512,128]{2,1,0:T(8,128)}, f32[1,512,128]{2,1,0:T(8,128)}) custom-call(f32[1,512,1024]{2,1,0:T(8,128)} %schur_hbm.1, f32[6,1,512]{2,1,0:T(1,128)} %bitcast.1, f32[1,512,128]{2,1,0:T(8,128)} %loads_hbm.1, s32[1,2]{1,0:T(1,128)} %sizes_hbm.1, s32[1,512]{1,0:T(1,128)} %contact_hbm.1, s32[1,512]{1,0:T(1,128)} %friction_hbm.1, ...), custom_call_target="tpu_custom_call" | custom-call | tf_op jit(solution)/shard_map/pallas_call | solution.py:479
  41.8 1.7 %copy.12 = f32[1,512,128]{2,1,0:T(8,128)} copy(f32[1,512,128]{2,1,0:T(8,128)} %get-tuple-element.4) | data formatting | bytes 524288
  43.5 1.7 %copy.13 = f32[1,512,128]{2,1,0:T(8,128)} copy(f32[1,512,128]{2,1,0:T(8,128)} %get-tuple-element.5) | data formatting | bytes 524288
